TPU v7x, 32 devices: a whole 2x2x4 slice. The times are simulated.
32 devices in a mesh: groups: 2 (over y), cells: 4 (over z), sub: 2 (over x), lev: 2 (over core).
Axes of the slice: x: 2, y: 2, z: 4, core: 2. Of those that a mesh axis runs over, the one named last changes fastest.
Arguments:
- tracers: float32 [2, 80, 8192], P(None, 'lev', ('groups', 'cells', 'sub')), parts along dimension 2, may hold values from -6 to 6
- thickness: float32 [80, 8192], P('lev', ('groups', 'cells', 'sub')), parts along dimension 1, may hold values from 0.5 to 1.5
- ssh: float32 [8192], P(('groups', 'cells', 'sub')), parts along dimension 0, may hold values from -3 to 3
- potential: float32 [8192], P(('groups', 'cells', 'sub')), parts along dimension 0, may hold values from -6 to 6
- neighbours: int32 [6, 4096], P(None, ('cells', 'sub')), may hold values from 0 to 640, as said below
- edge_weight: float32 [6, 4096], P(None, ('cells', 'sub')), may hold values from 0.5 to 2
- send_list: int32 [2, 512], P(None, ('cells', 'sub')), may hold values from 0 to 511
- remap_src: int32 [8192], P(('cells', 'sub')), may hold values from 0 to 511
- remap_owner: int32 [8192, 1], P(('cells', 'sub')), may hold values from 0 to 7; in each aligned block of 1024 rows (0 to 1023, 1024 to 2047, ...) at most 384 rows name the same one
- remap_local: int32 [8192], P(('cells', 'sub')), may hold values from 0 to 511
- remap_weight: float32 [8192], P(('cells', 'sub')), may hold values from 0.2 to 1
Outputs:
- tracers_new: float32 [2, 80, 8192], P(None, 'lev', ('groups', 'cells', 'sub')), parts along dimension 2
- thickness_new: float32 [80, 8192], P('lev', ('groups', 'cells', 'sub')), parts along dimension 1
- ssh_new: float32 [8192], P(('groups', 'cells', 'sub')), parts along dimension 0
- atm_flux: float32 [4, 8192], P(None, ('groups', 'cells', 'sub')), parts along dimension 1
There are 2 independent parts, one for each index of `groups`. A program takes and returns all parts, laid end to end along the dimension named above; an argument that names none is the same for every part. Nothing has to cross between parts.
Inputs may be any that keep to these rules, and one draw needn't show every extreme that they name: `neighbours`: A value below 512 is an owned cell, 512 + k the k-th cell of the previous partition's row 1 list, 576 + k the k-th cell of the next partition's row 0 list, and 640 an empty edge slot. `remap_owner`: the entries of one partition name each owner at most 384 times, and in every draw some partition names some owner exactly 384 times.
All inputs are finite; a program needn't handle non-finite values.
Results may differ from a plain program's by a relative error of at most 0.0003.
Values sent between devices are 32-bit elements; how exact they have to be, the bound alone decides.
A program may use at most 128 MiB of HBM per device.

v0:
```python
import jax
import jax.numpy as jnp
from jax import lax
from jax.sharding import PartitionSpec as P

LEV = 80
SUBCYCLES = 10
ATM_DEV = 512


thermal = 0.2
haline = 0.15
time_step = 0.05
mixing = 0.5
fast_step = 0.15


def carried_in(value, axis, join, neutral):
    count, mine = (lax.axis_size(axis), lax.axis_index(axis))
    pieces = lax.all_gather(value, axis)
    so_far = jnp.full_like(value, 0) + jnp.asarray(neutral, value.dtype)

    def step(position, so_far):
        longer = join(so_far, pieces[position])
        return jnp.where(position < mine, longer, so_far)

    return lax.fori_loop(0, count - 1, step, so_far)


def extended_2(block, sides, width):
    for axis, dim in sides:
        count = lax.axis_size(axis)
        forward = [(i, i + 1) for i in range(count - 1)]
        backward = [(target, source) for source, target in forward]
        low = lax.ppermute(
            lax.slice_in_dim(block, block.shape[dim] - width, None, axis=dim), axis, forward
        )
        high = lax.ppermute(lax.slice_in_dim(block, 0, width, axis=dim), axis, backward)
        block = jnp.concatenate([low, block, high], axis=dim)
    return block


def stencil(extended, neighbours, edge_weight):
    levels = extended.shape[0] // 4
    cell_count = neighbours.shape[1]
    blank_slot = extended.shape[1] - 1
    tracer_own = extended[: 2 * levels, :cell_count]
    height_own = extended[2 * levels : 3 * levels, :cell_count]
    mont_own = extended[3 * levels :, :cell_count]
    advect = jnp.zeros_like(tracer_own)
    laplace = jnp.zeros_like(tracer_own)
    height_rate = jnp.zeros_like(height_own)
    for edge_slot in range(neighbours.shape[0]):
        near_index = neighbours[edge_slot]
        coupling = edge_weight[edge_slot] * (near_index < blank_slot).astype(jnp.float32)
        gathered = extended[:, near_index]
        tracer_near = gathered[: 2 * levels]
        height_near = gathered[2 * levels : 3 * levels]
        mont_near = gathered[3 * levels :]
        normal_flow = -coupling[None, :] * (mont_near - mont_own)
        height_rate = height_rate - normal_flow * (0.5 * (height_near + height_own))
        both_flow = jnp.concatenate([normal_flow, normal_flow], axis=0)
        advect = advect - 0.5 * both_flow * (tracer_near - tracer_own)
        laplace = laplace + coupling[None, :] * (tracer_near - tracer_own)
    return (advect, laplace, height_rate)


def add_pair(earlier, later):
    return earlier + later


def per_device(
    tracers,
    thickness,
    ssh,
    potential,
    neighbours,
    edge_weight,
    send_list,
    remap_src,
    remap_owner,
    remap_local,
    remap_weight,
):
    levels = thickness.shape[0]
    cell_count = thickness.shape[1]
    halo_width = send_list.shape[1]
    old_tracers = tracers.reshape(2 * levels, cell_count)
    buoyancy = thermal * tracers[0] - haline * tracers[1]
    layer_load = buoyancy * thickness
    running = jnp.cumsum(layer_load, axis=0)
    above = carried_in(running[-1], "lev", add_pair, jnp.zeros_like(running[-1]))
    pressure = running + above[None, :] - 0.5 * layer_load
    montgomery = pressure + ssh[None, :]
    stacked = jnp.concatenate([old_tracers, thickness, montgomery], axis=0)
    packed = jnp.concatenate([stacked[:, send_list[0]], stacked[:, send_list[1]]], axis=1)
    received = extended_2(packed, ((("cells", "sub"), 1),), halo_width)
    extended = jnp.concatenate(
        [
            stacked,
            received[:, :halo_width],
            received[:, 3 * halo_width :],
            jnp.zeros((stacked.shape[0], 1), jnp.float32),
        ],
        axis=1,
    )
    advect, laplace, height_rate = stencil(extended, neighbours, edge_weight)
    new_tracers = old_tracers + time_step * (advect + mixing * laplace)
    provisional = thickness + time_step * height_rate
    columns = lax.psum(
        (
            jnp.sum(thickness * montgomery, axis=0),
            jnp.sum(provisional, axis=0),
            jnp.sum(provisional * new_tracers[:levels], axis=0),
            jnp.sum(provisional * new_tracers[levels:], axis=0),
            jnp.sum(new_tracers[:levels], axis=0),
            jnp.sum(new_tracers[levels:], axis=0),
        ),
        "lev",
    )
    forcing = columns[0] / LEV
    blank_slot = cell_count + 2 * halo_width
    coupling_all = edge_weight * (neighbours < blank_slot).astype(jnp.float32)
    slot_ids = jnp.arange(blank_slot + 1, dtype=jnp.int32)
    spread_table = jnp.zeros((blank_slot + 1, cell_count), jnp.float32)
    for edge_slot in range(neighbours.shape[0]):
        spread_table = (
            spread_table
            + (slot_ids[:, None] == neighbours[edge_slot][None, :]).astype(jnp.float32)
            * coupling_all[edge_slot][None, :]
        )
    coupling_total = jnp.sum(coupling_all, axis=0)
    send_flat = jnp.concatenate([send_list[0], send_list[1]])
    pick_table = (jnp.arange(cell_count, dtype=jnp.int32)[:, None] == send_flat[None, :]).astype(
        jnp.float32
    )

    def subcycle(step_index, state):
        potential_now, height_now = state
        potential_now = potential_now - fast_step * (height_now + forcing)
        outgoing = jnp.dot(potential_now, pick_table, precision=lax.Precision.HIGHEST)
        arrived = extended_2(outgoing, ((("cells", "sub"), 0),), halo_width)
        padded = jnp.concatenate(
            [
                potential_now,
                arrived[:halo_width],
                arrived[3 * halo_width :],
                jnp.zeros((1,), jnp.float32),
            ]
        )
        divergence = (
            jnp.dot(padded, spread_table, precision=lax.Precision.HIGHEST)
            - coupling_total * potential_now
        )
        return (potential_now, height_now + fast_step * divergence)

    potential_new, ssh_new = lax.fori_loop(0, SUBCYCLES, subcycle, (potential, ssh))
    correction = (LEV + ssh_new - columns[1]) / LEV
    thickness_new = provisional + correction[None, :]
    surface = jnp.stack(
        [
            ssh_new,
            potential_new,
            (columns[2] + correction * columns[4]) / LEV,
            (columns[3] + correction * columns[5]) / LEV,
        ]
    )
    contrib = remap_weight[None, :] * surface[:, remap_src]
    owners = remap_owner[:, 0]
    members = lax.axis_size(("cells", "sub"))
    dense_flux = (
        jnp.zeros((surface.shape[0], members * ATM_DEV), jnp.float32)
        .at[:, owners * ATM_DEV + remap_local]
        .add(contrib)
    )
    atm_flux = lax.psum_scatter(dense_flux, ("cells", "sub"), scatter_dimension=1, tiled=True)
    return (new_tracers.reshape(2, levels, cell_count), thickness_new, ssh_new, atm_flux)


def solution(mesh):
    placed = (
        P(None, "lev", ("groups", "cells", "sub")),
        P("lev", ("groups", "cells", "sub")),
        P(("groups", "cells", "sub")),
        P(("groups", "cells", "sub")),
        P(None, ("cells", "sub")),
        P(None, ("cells", "sub")),
        P(None, ("cells", "sub")),
        P(("cells", "sub")),
        P(("cells", "sub"), None),
        P(("cells", "sub")),
        P(("cells", "sub")),
    )
    return jax.shard_map(
        per_device,
        mesh=mesh,
        in_specs=placed,
        out_specs=(
            P(None, "lev", ("groups", "cells", "sub")),
            P("lev", ("groups", "cells", "sub")),
            P(("groups", "cells", "sub")),
            P(None, ("groups", "cells", "sub")),
        ),
        check_vma=False,
    )
```

profile of v0, /device:TPU:0, one launch (start us, length us, event | category | flops | bytes accessed | tf_op | source)
XLA Modules:
  0.0 236.4 jit_solution(18021261035098970296)
XLA Ops:
  9.0 1.9 all-gather
  13.9 4.7 %collective-permute-start.2 = (f32[160,64]{1,0:T(8,128)S(1)}, f32[160,64]{1,0:T(8,128)S(1)}, u32[]{:S(2)}, u32[]{:S(2)}) collective-permute-start(f32[160,64]{1,0:T(8,128)S(1)} %bitcast.116), channel_id=1, source_target_pairs={{0,2},{2,4},{4,6},{6,8},{8,10},{10,12},{12,14},{1,3},{3,5},{5,7},{... | collective-permute-start | bytes 122888 | tf_op jit(solution)/shard_map/ppermute | solution.py:35
  21.1 4.6 %collective-permute-done.3 = f32[160,64]{1,0:T(8,128)S(1)} collective-permute-done((f32[160,64]{1,0:T(8,128)S(1)}, f32[160,64]{1,0:T(8,128)S(1)}, u32[]{:S(2)}, u32[]{:S(2)}) %collective-permute-start.3) | collective-permute-done | bytes 40992 | tf_op jit(solution)/shard_map/ppermute | solution.py:38
  37.1 3.3 %all-reduce = (f32[512]{0:T(512)S(1)}, f32[512]{0:T(512)S(1)}, f32[512]{0:T(512)S(1)}, f32[512]{0:T(512)S(1)}, f32[512]{0:T(512)S(1)}, /*index=5*/f32[512]{0:T(512)S(1)}) all-reduce(f32[512]{0:T(512)S(1)} %get-tuple-element.129, f32[512]{0:T(512)S(1)} %get-tuple-element.176, ...), channel_id=1, replica_groups=mesh['groups'=2,'cells'=4,'sub'=2,'lev'=2] {'lev'}, use_global_device_ids=true, to_apply=%region_7.8 | all-reduce | flops 3072 | bytes 24576 | tf_op jit(solution)/shard_map/psum | solution.py:110
  40.4 102.7 %while.3 = (s32[]{:T(128)}, f32[512]{0:T(512)S(1)}, f32[512]{0:T(512)S(1)}, f32[512]{0:T(512)S(1)}, f32[512]{0:T(512)S(1)}, /*index=5*/s32[128]{0:T(128)S(1)}, s...) while((s32[]{:T(128)}, f32[512]{0:T(512)S(1)}, ...), condition=%wide.region_5.6_spmd.clone, body=%wide.region_4.5_spmd.clone.sunk | while | flops 10440581 | bytes 64281 | solution.py:157
  42.1 5.0 %collective-permute-start.1 = (f32[64]{0:T(128)S(1)}, f32[64]{0:T(128)S(1)}, u32[]{:S(2)}, u32[]{:S(2)}) collective-permute-start(f32[64]{0:T(128)S(1)} %get-tuple-element.347), channel_id=1, source_target_pairs={{0,2},{2,4},{4,6},{6,8},{8,10},{10,12},{12,14},{1,3},{3,5},{5,7},{... | collective-permute-start | bytes 776 | tf_op jit(solution)/shard_map/while/body/eval_jaxpr/ppermute | solution.py:35
  48.4 1.6 fusion.105
  51.7 5.4 %collective-permute-start.1 = (f32[64]{0:T(128)S(1)}, f32[64]{0:T(128)S(1)}, u32[]{:S(2)}, u32[]{:S(2)}) collective-permute-start(f32[64]{0:T(128)S(1)} %get-tuple-element.347), channel_id=1, source_target_pairs={{0,2},{2,4},{4,6},{6,8},{8,10},{10,12},{12,14},{1,3},{3,5},{5,7},{... | collective-permute-start | bytes 776 | tf_op jit(solution)/shard_map/while/body/eval_jaxpr/ppermute | solution.py:35
  61.8 5.7 %collective-permute-start.1 = (f32[64]{0:T(128)S(1)}, f32[64]{0:T(128)S(1)}, u32[]{:S(2)}, u32[]{:S(2)}) collective-permute-start(f32[64]{0:T(128)S(1)} %get-tuple-element.347), channel_id=1, source_target_pairs={{0,2},{2,4},{4,6},{6,8},{8,10},{10,12},{12,14},{1,3},{3,5},{5,7},{... | collective-permute-start | bytes 776 | tf_op jit(solution)/shard_map/while/body/eval_jaxpr/ppermute | solution.py:35
  68.9 1.6 fusion.105
  72.2 5.7 %collective-permute-start.1 = (f32[64]{0:T(128)S(1)}, f32[64]{0:T(128)S(1)}, u32[]{:S(2)}, u32[]{:S(2)}) collective-permute-start(f32[64]{0:T(128)S(1)} %get-tuple-element.347), channel_id=1, source_target_pairs={{0,2},{2,4},{4,6},{6,8},{8,10},{10,12},{12,14},{1,3},{3,5},{5,7},{... | collective-permute-start | bytes 776 | tf_op jit(solution)/shard_map/while/body/eval_jaxpr/ppermute | solution.py:35
  79.2 1.6 fusion.105
  82.6 5.7 %collective-permute-start.1 = (f32[64]{0:T(128)S(1)}, f32[64]{0:T(128)S(1)}, u32[]{:S(2)}, u32[]{:S(2)}) collective-permute-start(f32[64]{0:T(128)S(1)} %get-tuple-element.347), channel_id=1, source_target_pairs={{0,2},{2,4},{4,6},{6,8},{8,10},{10,12},{12,14},{1,3},{3,5},{5,7},{... | collective-permute-start | bytes 776 | tf_op jit(solution)/shard_map/while/body/eval_jaxpr/ppermute | solution.py:35
  89.6 1.6 fusion.105
  92.9 5.7 %collective-permute-start.1 = (f32[64]{0:T(128)S(1)}, f32[64]{0:T(128)S(1)}, u32[]{:S(2)}, u32[]{:S(2)}) collective-permute-start(f32[64]{0:T(128)S(1)} %get-tuple-element.347), channel_id=1, source_target_pairs={{0,2},{2,4},{4,6},{6,8},{8,10},{10,12},{12,14},{1,3},{3,5},{5,7},{... | collective-permute-start | bytes 776 | tf_op jit(solution)/shard_map/while/body/eval_jaxpr/ppermute | solution.py:35
  100.0 1.6 fusion.105
  103.3 5.7 %collective-permute-start.1 = (f32[64]{0:T(128)S(1)}, f32[64]{0:T(128)S(1)}, u32[]{:S(2)}, u32[]{:S(2)}) collective-permute-start(f32[64]{0:T(128)S(1)} %get-tuple-element.347), channel_id=1, source_target_pairs={{0,2},{2,4},{4,6},{6,8},{8,10},{10,12},{12,14},{1,3},{3,5},{5,7},{... | collective-permute-start | bytes 776 | tf_op jit(solution)/shard_map/while/body/eval_jaxpr/ppermute | solution.py:35
  110.3 1.6 fusion.105
  113.6 5.7 %collective-permute-start.1 = (f32[64]{0:T(128)S(1)}, f32[64]{0:T(128)S(1)}, u32[]{:S(2)}, u32[]{:S(2)}) collective-permute-start(f32[64]{0:T(128)S(1)} %get-tuple-element.347), channel_id=1, source_target_pairs={{0,2},{2,4},{4,6},{6,8},{8,10},{10,12},{12,14},{1,3},{3,5},{5,7},{... | collective-permute-start | bytes 776 | tf_op jit(solution)/shard_map/while/body/eval_jaxpr/ppermute | solution.py:35
  124.0 5.7 %collective-permute-start.1 = (f32[64]{0:T(128)S(1)}, f32[64]{0:T(128)S(1)}, u32[]{:S(2)}, u32[]{:S(2)}) collective-permute-start(f32[64]{0:T(128)S(1)} %get-tuple-element.347), channel_id=1, source_target_pairs={{0,2},{2,4},{4,6},{6,8},{8,10},{10,12},{12,14},{1,3},{3,5},{5,7},{... | collective-permute-start | bytes 776 | tf_op jit(solution)/shard_map/while/body/eval_jaxpr/ppermute | solution.py:35
  134.4 5.7 %collective-permute-start.1 = (f32[64]{0:T(128)S(1)}, f32[64]{0:T(128)S(1)}, u32[]{:S(2)}, u32[]{:S(2)}) collective-permute-start(f32[64]{0:T(128)S(1)} %get-tuple-element.347), channel_id=1, source_target_pairs={{0,2},{2,4},{4,6},{6,8},{8,10},{10,12},{12,14},{1,3},{3,5},{5,7},{... | collective-permute-start | bytes 776 | tf_op jit(solution)/shard_map/while/body/eval_jaxpr/ppermute | solution.py:35
  143.3 10.7 %scatter_custom_fusion = f32[4,4096]{0,1:T(8,128)} fusion(s32[1024]{0:T(1024)S(1)} %get-tuple-element.233, f32[]{:T(128)} %constant.29.clone.1, f32[1024]{0:T(1024)S(1)} %copy-done.7, f32[4,512]{0,1:T(8,128)S(1)} %copy.69, s32[1024]{0:T(1024)S(1)} %get-tuple-element.234), kind=kCustom, calls=%fused_computation.51 | custom fusion | flops 8192 | bytes 335876 | tf_op jit(solution)/shard_map/scatter-add | solution.py:174
  154.6 73.3 %reduce-scatter.2.cloned.1.call-done = f32[4,512]{0,1:T(8,128)} async-done(((f32[4,4096]{0,1:T(8,128)}), f32[4,512]{0,1:T(8,128)}) %reduce-scatter.2.cloned.1.call-update) | async-done | bytes 8208 | tf_op jit(solution)/shard_map/reduce_scatter | solution.py:176
  227.9 1.7 copy.70
  (175 shorter events, 55.7 us)
Async XLA Ops:
  7.2 220.8 %reduce-scatter.2.cloned.1.call-start = ((), (), s32[]{:S(2)}) async-start(), calls=%async_computation.1 | async-start | bytes 2359296 | tf_op jit(solution)/shard_map/reduce_scatter | solution.py:176
  13.9 7.1 %collective-permute-start.2 = (f32[160,64]{1,0:T(8,128)S(1)}, f32[160,64]{1,0:T(8,128)S(1)}, u32[]{:S(2)}, u32[]{:S(2)}) collective-permute-start(f32[160,64]{1,0:T(8,128)S(1)} %bitcast.116), channel_id=1, source_target_pairs={{0,2},{2,4},{4,6},{6,8},{8,10},{10,12},{12,14},{1,3},{3,5},{5,7},{... | collective-permute-start | bytes 122888 | tf_op jit(solution)/shard_map/ppermute | solution.py:35
  19.4 6.3 %collective-permute-start.3 = (f32[160,64]{1,0:T(8,128)S(1)}, f32[160,64]{1,0:T(8,128)S(1)}, u32[]{:S(2)}, u32[]{:S(2)}) collective-permute-start(f32[160,64]{1,0:T(8,128)S(1)} %bitcast.117), channel_id=1, source_target_pairs={{2,0},{4,2},{6,4},{8,6},{10,8},{12,10},{14,12},{3,1},{5,3},{7,5},{... | collective-permute-start | bytes 122888 | tf_op jit(solution)/shard_map/ppermute | solution.py:38
  40.4 102.9 %copy-start.7 = (f32[1024]{0:T(1024)S(1)}, f32[1024]{0:T(1024)}, u32[]{:S(2)}) copy-start(f32[1024]{0:T(1024)} %param.23) | copy-start | bytes 12292
  40.7 6.3 %collective-permute-start = (f32[64]{0:T(128)S(1)}, f32[64]{0:T(128)S(1)}, u32[]{:S(2)}, u32[]{:S(2)}) collective-permute-start(f32[64]{0:T(128)S(1)} %get-tuple-element.346), channel_id=1, source_target_pairs={{2,0},{4,2},{6,4},{8,6},{10,8},{12,10},{14,12},{3,1},{5,3},{7,5},{... | collective-permute-start | bytes 776 | tf_op jit(solution)/shard_map/while/body/eval_jaxpr/ppermute | solution.py:38
  42.1 6.3 %collective-permute-start.1 = (f32[64]{0:T(128)S(1)}, f32[64]{0:T(128)S(1)}, u32[]{:S(2)}, u32[]{:S(2)}) collective-permute-start(f32[64]{0:T(128)S(1)} %get-tuple-element.347), channel_id=1, source_target_pairs={{0,2},{2,4},{4,6},{6,8},{8,10},{10,12},{12,14},{1,3},{3,5},{5,7},{... | collective-permute-start | bytes 776 | tf_op jit(solution)/shard_map/while/body/eval_jaxpr/ppermute | solution.py:35
  50.4 6.8 %collective-permute-start = (f32[64]{0:T(128)S(1)}, f32[64]{0:T(128)S(1)}, u32[]{:S(2)}, u32[]{:S(2)}) collective-permute-start(f32[64]{0:T(128)S(1)} %get-tuple-element.346), channel_id=1, source_target_pairs={{2,0},{4,2},{6,4},{8,6},{10,8},{12,10},{14,12},{3,1},{5,3},{7,5},{... | collective-permute-start | bytes 776 | tf_op jit(solution)/shard_map/while/body/eval_jaxpr/ppermute | solution.py:38
  51.7 6.7 %collective-permute-start.1 = (f32[64]{0:T(128)S(1)}, f32[64]{0:T(128)S(1)}, u32[]{:S(2)}, u32[]{:S(2)}) collective-permute-start(f32[64]{0:T(128)S(1)} %get-tuple-element.347), channel_id=1, source_target_pairs={{0,2},{2,4},{4,6},{6,8},{8,10},{10,12},{12,14},{1,3},{3,5},{5,7},{... | collective-permute-start | bytes 776 | tf_op jit(solution)/shard_map/while/body/eval_jaxpr/ppermute | solution.py:35
  60.5 7.0 %collective-permute-start = (f32[64]{0:T(128)S(1)}, f32[64]{0:T(128)S(1)}, u32[]{:S(2)}, u32[]{:S(2)}) collective-permute-start(f32[64]{0:T(128)S(1)} %get-tuple-element.346), channel_id=1, source_target_pairs={{2,0},{4,2},{6,4},{8,6},{10,8},{12,10},{14,12},{3,1},{5,3},{7,5},{... | collective-permute-start | bytes 776 | tf_op jit(solution)/shard_map/while/body/eval_jaxpr/ppermute | solution.py:38
  61.8 7.0 %collective-permute-start.1 = (f32[64]{0:T(128)S(1)}, f32[64]{0:T(128)S(1)}, u32[]{:S(2)}, u32[]{:S(2)}) collective-permute-start(f32[64]{0:T(128)S(1)} %get-tuple-element.347), channel_id=1, source_target_pairs={{0,2},{2,4},{4,6},{6,8},{8,10},{10,12},{12,14},{1,3},{3,5},{5,7},{... | collective-permute-start | bytes 776 | tf_op jit(solution)/shard_map/while/body/eval_jaxpr/ppermute | solution.py:35
  70.9 7.0 %collective-permute-start = (f32[64]{0:T(128)S(1)}, f32[64]{0:T(128)S(1)}, u32[]{:S(2)}, u32[]{:S(2)}) collective-permute-start(f32[64]{0:T(128)S(1)} %get-tuple-element.346), channel_id=1, source_target_pairs={{2,0},{4,2},{6,4},{8,6},{10,8},{12,10},{14,12},{3,1},{5,3},{7,5},{... | collective-permute-start | bytes 776 | tf_op jit(solution)/shard_map/while/body/eval_jaxpr/ppermute | solution.py:38
  72.2 7.0 %collective-permute-start.1 = (f32[64]{0:T(128)S(1)}, f32[64]{0:T(128)S(1)}, u32[]{:S(2)}, u32[]{:S(2)}) collective-permute-start(f32[64]{0:T(128)S(1)} %get-tuple-element.347), channel_id=1, source_target_pairs={{0,2},{2,4},{4,6},{6,8},{8,10},{10,12},{12,14},{1,3},{3,5},{5,7},{... | collective-permute-start | bytes 776 | tf_op jit(solution)/shard_map/while/body/eval_jaxpr/ppermute | solution.py:35
  81.3 7.0 %collective-permute-start = (f32[64]{0:T(128)S(1)}, f32[64]{0:T(128)S(1)}, u32[]{:S(2)}, u32[]{:S(2)}) collective-permute-start(f32[64]{0:T(128)S(1)} %get-tuple-element.346), channel_id=1, source_target_pairs={{2,0},{4,2},{6,4},{8,6},{10,8},{12,10},{14,12},{3,1},{5,3},{7,5},{... | collective-permute-start | bytes 776 | tf_op jit(solution)/shard_map/while/body/eval_jaxpr/ppermute | solution.py:38
  82.6 7.0 %collective-permute-start.1 = (f32[64]{0:T(128)S(1)}, f32[64]{0:T(128)S(1)}, u32[]{:S(2)}, u32[]{:S(2)}) collective-permute-start(f32[64]{0:T(128)S(1)} %get-tuple-element.347), channel_id=1, source_target_pairs={{0,2},{2,4},{4,6},{6,8},{8,10},{10,12},{12,14},{1,3},{3,5},{5,7},{... | collective-permute-start | bytes 776 | tf_op jit(solution)/shard_map/while/body/eval_jaxpr/ppermute | solution.py:35
  91.6 7.0 %collective-permute-start = (f32[64]{0:T(128)S(1)}, f32[64]{0:T(128)S(1)}, u32[]{:S(2)}, u32[]{:S(2)}) collective-permute-start(f32[64]{0:T(128)S(1)} %get-tuple-element.346), channel_id=1, source_target_pairs={{2,0},{4,2},{6,4},{8,6},{10,8},{12,10},{14,12},{3,1},{5,3},{7,5},{... | collective-permute-start | bytes 776 | tf_op jit(solution)/shard_map/while/body/eval_jaxpr/ppermute | solution.py:38
  92.9 7.0 %collective-permute-start.1 = (f32[64]{0:T(128)S(1)}, f32[64]{0:T(128)S(1)}, u32[]{:S(2)}, u32[]{:S(2)}) collective-permute-start(f32[64]{0:T(128)S(1)} %get-tuple-element.347), channel_id=1, source_target_pairs={{0,2},{2,4},{4,6},{6,8},{8,10},{10,12},{12,14},{1,3},{3,5},{5,7},{... | collective-permute-start | bytes 776 | tf_op jit(solution)/shard_map/while/body/eval_jaxpr/ppermute | solution.py:35
  102.0 7.0 %collective-permute-start = (f32[64]{0:T(128)S(1)}, f32[64]{0:T(128)S(1)}, u32[]{:S(2)}, u32[]{:S(2)}) collective-permute-start(f32[64]{0:T(128)S(1)} %get-tuple-element.346), channel_id=1, source_target_pairs={{2,0},{4,2},{6,4},{8,6},{10,8},{12,10},{14,12},{3,1},{5,3},{7,5},{... | collective-permute-start | bytes 776 | tf_op jit(solution)/shard_map/while/body/eval_jaxpr/ppermute | solution.py:38
  103.3 7.0 %collective-permute-start.1 = (f32[64]{0:T(128)S(1)}, f32[64]{0:T(128)S(1)}, u32[]{:S(2)}, u32[]{:S(2)}) collective-permute-start(f32[64]{0:T(128)S(1)} %get-tuple-element.347), channel_id=1, source_target_pairs={{0,2},{2,4},{4,6},{6,8},{8,10},{10,12},{12,14},{1,3},{3,5},{5,7},{... | collective-permute-start | bytes 776 | tf_op jit(solution)/shard_map/while/body/eval_jaxpr/ppermute | solution.py:35
  112.3 7.0 %collective-permute-start = (f32[64]{0:T(128)S(1)}, f32[64]{0:T(128)S(1)}, u32[]{:S(2)}, u32[]{:S(2)}) collective-permute-start(f32[64]{0:T(128)S(1)} %get-tuple-element.346), channel_id=1, source_target_pairs={{2,0},{4,2},{6,4},{8,6},{10,8},{12,10},{14,12},{3,1},{5,3},{7,5},{... | collective-permute-start | bytes 776 | tf_op jit(solution)/shard_map/while/body/eval_jaxpr/ppermute | solution.py:38
  113.6 7.0 %collective-permute-start.1 = (f32[64]{0:T(128)S(1)}, f32[64]{0:T(128)S(1)}, u32[]{:S(2)}, u32[]{:S(2)}) collective-permute-start(f32[64]{0:T(128)S(1)} %get-tuple-element.347), channel_id=1, source_target_pairs={{0,2},{2,4},{4,6},{6,8},{8,10},{10,12},{12,14},{1,3},{3,5},{5,7},{... | collective-permute-start | bytes 776 | tf_op jit(solution)/shard_map/while/body/eval_jaxpr/ppermute | solution.py:35
  122.7 7.0 %collective-permute-start = (f32[64]{0:T(128)S(1)}, f32[64]{0:T(128)S(1)}, u32[]{:S(2)}, u32[]{:S(2)}) collective-permute-start(f32[64]{0:T(128)S(1)} %get-tuple-element.346), channel_id=1, source_target_pairs={{2,0},{4,2},{6,4},{8,6},{10,8},{12,10},{14,12},{3,1},{5,3},{7,5},{... | collective-permute-start | bytes 776 | tf_op jit(solution)/shard_map/while/body/eval_jaxpr/ppermute | solution.py:38
  124.0 7.0 %collective-permute-start.1 = (f32[64]{0:T(128)S(1)}, f32[64]{0:T(128)S(1)}, u32[]{:S(2)}, u32[]{:S(2)}) collective-permute-start(f32[64]{0:T(128)S(1)} %get-tuple-element.347), channel_id=1, source_target_pairs={{0,2},{2,4},{4,6},{6,8},{8,10},{10,12},{12,14},{1,3},{3,5},{5,7},{... | collective-permute-start | bytes 776 | tf_op jit(solution)/shard_map/while/body/eval_jaxpr/ppermute | solution.py:35
  133.1 7.0 %collective-permute-start = (f32[64]{0:T(128)S(1)}, f32[64]{0:T(128)S(1)}, u32[]{:S(2)}, u32[]{:S(2)}) collective-permute-start(f32[64]{0:T(128)S(1)} %get-tuple-element.346), channel_id=1, source_target_pairs={{2,0},{4,2},{6,4},{8,6},{10,8},{12,10},{14,12},{3,1},{5,3},{7,5},{... | collective-permute-start | bytes 776 | tf_op jit(solution)/shard_map/while/body/eval_jaxpr/ppermute | solution.py:38
  134.4 6.9 %collective-permute-start.1 = (f32[64]{0:T(128)S(1)}, f32[64]{0:T(128)S(1)}, u32[]{:S(2)}, u32[]{:S(2)}) collective-permute-start(f32[64]{0:T(128)S(1)} %get-tuple-element.347), channel_id=1, source_target_pairs={{0,2},{2,4},{4,6},{6,8},{8,10},{10,12},{12,14},{1,3},{3,5},{5,7},{... | collective-permute-start | bytes 776 | tf_op jit(solution)/shard_map/while/body/eval_jaxpr/ppermute | solution.py:35
  (11 other events, 89.6 us)
Sparse Core Ops, SparseCore 0:
  154.1 73.7 reduce-scatter.1
where the time goes:
time: 237 us; the launch traced here: 236 us
  waiting for transfers between devices  90.7 us (38%)
  starting transfers between devices  74.8 us (32%)
  matrix products  19 us (8%)
  other arithmetic  16.2 us (7%)
  local copies, waits for them, and re-layouts  15.8 us (7%)
  between operations  14.5 us (6%)
  blocking collectives  5.22 us (2%)
    reduce_scatter x1, waiting for transfers between devices, per_device(): lax.psum_scatter(dense_flux, ('cells', 'sub'), scatter_dimension=1, tiled...  73.3 us
    ppermute x11, starting transfers between devices, extended_2(): lax.ppermute(lax.slice_in_dim(block, block.shape[dim] - width, None, axis...  60.5 us
    dot_general x10, matrix products, subcycle(): jnp.dot(padded, spread_table, precision=lax.Precision.HIGHEST)  16.5 us
    ppermute x11, starting transfers between devices, extended_2(): lax.ppermute(lax.slice_in_dim(block, 0, width, axis=dim), axis, backward)  14.2 us
    ppermute x11, waiting for transfers between devices, extended_2(): lax.ppermute(lax.slice_in_dim(block, block.shape[dim] - width, None, axis...  12.7 us
    scatter-add x1, other arithmetic, per_device(): dense_flux = jnp.zeros((surface.shape[0], members * ATM_DEV), jnp.float32...  10.7 us
    gather x12, local copies, waits for them, and re-layouts, stencil(): gathered = extended[:, near_index]  10.5 us
  transfers between devices with their start and end apart: 23, of which 12 were waited for; matrix products, arithmetic and copies ran while one was open for 1% of the time, Pallas kernels for 0%

commit v1 on v0

v1 whole, which is shorter than its diff:
```python
import functools

import jax
import jax.numpy as jnp
from jax import lax
from jax.experimental import pallas as pl
from jax.experimental.pallas import tpu as pltpu
from jax.sharding import PartitionSpec as P

SUBCYCLES = 10

thermal = 0.2
haline = 0.15
time_step = 0.05
mixing = 0.5
fast_step = 0.15

F32 = jnp.float32
BF16 = jnp.bfloat16
LANES = 128


def repeat(count, body):
    if count <= 16:
        for i in range(count):
            body(i)
    else:

        def step(i, carry):
            body(i)
            return carry

        lax.fori_loop(0, count, step, 0)


def guarded(flag, body):
    if flag is True:
        body()
    else:
        pl.when(flag)(body)


def split(x):
    high = x.astype(BF16)
    return high, (x - high.astype(F32)).astype(BF16)


def lanes_of(x, index):
    return jnp.take_along_axis(x, index, axis=1, mode="promise_in_bounds")


def ocean_kernel(
    n_cells,
    n_sub,
    reach,
    window,
    tr_ref,
    th_ref,
    ssh_ref,
    pot_ref,
    near_ref,
    ew_ref,
    send_ref,
    src_ref,
    own_ref,
    loc_ref,
    rw_ref,
    tr_out,
    th_out,
    ssh_out,
    atm_out,
    halo_send,
    halo_recv,
    table_all,
    state_mine,
    state_all,
    col_mine,
    col_other,
    flux_send,
    flux_recv,
    x_all,
    x_split,
    hot,
    prov_ref,
    flux_lhs,
    flux_hot,
    halo_ss,
    halo_rs,
    table_ss,
    table_rs,
    state_ss,
    state_rs,
    col_ss,
    col_rs,
    flux_ss,
    flux_rs,
):
    members = n_cells * n_sub
    levels, cells = th_ref.shape
    edges = near_ref.shape[0]
    chunks = cells // LANES
    halo = send_ref.shape[1] // 2
    full_levels = 2 * levels
    q = lax.axis_index("cells") * n_sub + lax.axis_index("sub")
    lev = lax.axis_index("lev")
    whole = window == members

    def at(p, level):
        return {"cells": lax.div(p, n_sub), "sub": lax.rem(p, n_sub), "lev": level}

    def slot_of(source, target):
        return source if whole else source - target + reach

    mine = slot_of(q, q)

    def window_partner(i):
        if whole:
            return lax.rem(q + i, members), True
        d = i - reach
        p = q + d
        ok = (p >= 0) & (p < members)
        return jnp.clip(p, 0, members - 1), ok

    same = range(1, members) if whole else [i for i in range(window) if i != reach]
    both = range(window)

    barrier = pltpu.get_barrier_semaphore()

    def greet(i):
        p = lax.rem(q + 1 + i, members)
        pl.semaphore_signal(
            barrier, inc=1, device_id=at(p, lev), device_id_type=pl.DeviceIdType.MESH
        )

    repeat(members - 1, greet)
    for i in both:
        p, ok = window_partner(i)
        guarded(
            ok,
            lambda p=p: pl.semaphore_signal(
                barrier, inc=1, device_id=at(p, 1 - lev), device_id_type=pl.DeviceIdType.MESH
            ),
        )
    if whole:
        greetings = members - 1 + window
    else:
        greetings = (
            members
            - 1
            + jnp.minimum(q + reach, members - 1)
            - jnp.maximum(q - reach, 0)
            + 1
        )

    row8 = lax.broadcasted_iota(jnp.int32, (8, LANES), 0)
    lane8 = lax.broadcasted_iota(jnp.int32, (8, LANES), 1)
    upper = row8 < 4
    chunk8 = jnp.where(upper, row8, row8 - 4)
    left8 = lane8 < halo

    def pair(v):
        r = pltpu.roll(v, 4, 0)
        return jnp.where(upper, v, r), jnp.where(upper, r, v)

    def put_rows(ref, start, row):
        for c in range(chunks):
            ref[start + c : start + c + 1, :] = row[:, c * LANES : (c + 1) * LANES]

    temp = tr_ref[0]
    salt = tr_ref[1]
    thick = th_ref[...]
    load = (thermal * temp - haline * salt) * thick
    rows = lax.broadcasted_iota(jnp.int32, (levels, levels), 0)
    cols = lax.broadcasted_iota(jnp.int32, (levels, levels), 1)
    below = jnp.where(cols < rows, 1.0, jnp.where(cols == rows, 0.5, 0.0)).astype(F32)
    pressure = lax.dot_general(
        below,
        load,
        (((1,), (0,)), ((), ())),
        precision=lax.Precision.HIGHEST,
        preferred_element_type=F32,
    )
    ssh_row = jnp.concatenate([ssh_ref[c : c + 1, :] for c in range(chunks)], axis=1)
    part_mont = pressure + ssh_row
    x_all[0:levels, 0:cells] = temp
    x_all[levels : 2 * levels, 0:cells] = salt
    x_all[2 * levels : 3 * levels, 0:cells] = thick
    x_all[3 * levels : 4 * levels, 0:cells] = part_mont

    state_mine[0:4, :] = ssh_ref[...]
    state_mine[4:8, :] = pot_ref[...]
    put_rows(state_mine, 8, jnp.sum(thick * part_mont, axis=0, keepdims=True))
    put_rows(state_mine, 12, jnp.sum(load, axis=0, keepdims=True))
    put_rows(state_mine, 16, jnp.sum(thick, axis=0, keepdims=True))
    state_mine[20:24, :] = jnp.zeros((4, LANES), F32)

    my_table = table_all.at[mine]
    blank_slot = cells + 2 * halo
    for e in range(edges):
        index_row = near_ref[e : e + 1, :]
        weight = jnp.where(index_row < blank_slot, ew_ref[e : e + 1, :], 0.0)
        put_rows(my_table, e * 4, index_row.astype(F32))
        put_rows(my_table, edges * 4 + e * 4, weight)
    my_table[8 * edges : 8 * edges + 8, :] = jnp.broadcast_to(
        send_ref[...].astype(F32), (8, LANES)
    )

    pick = (
        (
            lax.broadcasted_iota(jnp.int32, (cells, LANES), 0)
            == jnp.broadcast_to(send_ref[...], (cells, LANES))
        )
        .astype(F32)
        .astype(BF16)
    )
    own_high, own_low = split(x_all[:, 0:cells])
    picked = jnp.dot(own_high, pick, preferred_element_type=F32) + jnp.dot(
        own_low, pick, preferred_element_type=F32
    )
    first, second = picked[: 2 * levels], picked[2 * levels :]
    left_wide = lax.broadcasted_iota(jnp.int32, (2 * levels, LANES), 1) < halo
    halo_send[1] = jnp.where(left_wide, first, pltpu.roll(second, halo, 1))
    halo_send[0] = jnp.where(left_wide, pltpu.roll(first, halo, 1), second)

    has_prev = q > 0
    has_next = q < members - 1
    prev_q = jnp.maximum(q - 1, 0)
    next_q = jnp.minimum(q + 1, members - 1)

    pl.semaphore_wait(barrier, greetings)

    def halo_copy(side, target):
        return pltpu.make_async_remote_copy(
            src_ref=halo_send.at[side],
            dst_ref=halo_recv.at[1 - side],
            send_sem=halo_ss.at[side],
            recv_sem=halo_rs.at[1 - side],
            device_id=at(target, lev),
            device_id_type=pl.DeviceIdType.MESH,
        )

    pl.when(has_prev)(lambda: halo_copy(0, prev_q).start())
    pl.when(has_next)(lambda: halo_copy(1, next_q).start())

    def state_copy(i, level, other):
        p, ok = window_partner(i)
        return (
            pltpu.make_async_remote_copy(
                src_ref=state_mine,
                dst_ref=state_all.at[lev, slot_of(q, p)],
                send_sem=state_ss.at[other, i],
                recv_sem=state_rs.at[lev, slot_of(q, p)],
                device_id=at(p, level),
                device_id_type=pl.DeviceIdType.MESH,
            ),
            ok,
        )

    def table_copy(i):
        p, ok = window_partner(i)
        return (
            pltpu.make_async_remote_copy(
                src_ref=table_all.at[mine],
                dst_ref=table_all.at[slot_of(q, p)],
                send_sem=table_ss.at[i],
                recv_sem=table_rs.at[slot_of(q, p)],
                device_id=at(p, lev),
                device_id_type=pl.DeviceIdType.MESH,
            ),
            ok,
        )

    sends = (
        [state_copy(i, 1 - lev, 1) for i in both]
        + [state_copy(i, lev, 0) for i in same]
        + [table_copy(i) for i in same]
    )
    for copy, ok in sends:
        guarded(ok, copy.start)

    state_all[lev, mine] = state_mine[...]

    for e in range(edges):
        for k in range(x_all.shape[1] // LANES):
            ids = lax.broadcasted_iota(jnp.int32, (LANES, cells), 0) + k * LANES
            hot[e, k * LANES : (k + 1) * LANES, :] = (
                (ids == jnp.broadcast_to(near_ref[e : e + 1, :], (LANES, cells)))
                .astype(F32)
                .astype(BF16)
            )
    entry_rows = src_ref.shape[0]
    low_ids = lax.broadcasted_iota(jnp.int32, (LANES, LANES), 0)
    for k in range(entry_rows):
        low = jnp.bitwise_and(loc_ref[k : k + 1, :], LANES - 1)
        flux_hot[:, k * LANES : (k + 1) * LANES] = (
            (low_ids == jnp.broadcast_to(low, (LANES, LANES))).astype(F32).astype(BF16)
        )

    def slot_exists(s):
        if whole:
            return True
        p = q + s - reach
        return (p >= 0) & (p < members)

    pl.when(has_prev)(lambda: halo_copy(1, prev_q).wait_recv())
    pl.when(has_next)(lambda: halo_copy(0, next_q).wait_recv())

    def wait_state(level, s, skip):
        def body():
            pltpu.make_async_remote_copy(
                src_ref=state_mine,
                dst_ref=state_all.at[level, s],
                send_sem=state_ss.at[0, 0],
                recv_sem=state_rs.at[level, s],
                device_id=at(q, 1 - lev),
                device_id_type=pl.DeviceIdType.MESH,
            ).wait_recv()

        ok = slot_exists(s)
        if skip:
            keep = s != mine
            ok = keep if ok is True else keep & ok
        guarded(ok, body)

    for s in range(window):
        wait_state(1 - lev, s, False)
    for s in range(window):
        wait_state(lev, s, True)

    lower_level = lev == 1

    def total_of(slot):
        return pair(state_all[0, slot, 8:16, :])[1]

    def take_listed(value, list_row):
        low = jnp.bitwise_and(list_row, LANES - 1)
        high = jnp.right_shift(list_row, 7)
        got = lanes_of(value, low)
        got = jnp.where(upper & (high == chunk8), got, 0.0)
        return jnp.sum(got, axis=0, keepdims=True)

    def wait_table(s):
        def body():
            pltpu.make_async_remote_copy(
                src_ref=table_all.at[mine],
                dst_ref=table_all.at[s],
                send_sem=table_ss.at[0],
                recv_sem=table_rs.at[s],
                device_id=at(q, 1 - lev),
                device_id_type=pl.DeviceIdType.MESH,
            ).wait_recv()

        ok = slot_exists(s)
        keep = s != mine
        guarded(keep if ok is True else keep & ok, body)

    for s in range(window):
        wait_table(s)

    def list_of(slot):
        return table_all[slot, 8 * edges : 8 * edges + 8, :].astype(jnp.int32)

    above_mine = jnp.where(lower_level, total_of(mine), 0.0)
    above_row = jnp.concatenate([above_mine[c : c + 1, :] for c in range(chunks)], axis=1)
    prev_slot = slot_of(prev_q, q)
    next_slot = slot_of(next_q, q)
    above_halo = jnp.where(
        left8[0:1],
        jnp.where(has_prev, take_listed(total_of(prev_slot), list_of(prev_slot)), 0.0),
        jnp.where(has_next, take_listed(total_of(next_slot), list_of(next_slot)), 0.0),
    )
    above_halo = jnp.where(lower_level, above_halo, 0.0)

    from_prev = jnp.where(has_prev, halo_recv[0], 0.0)
    from_next = jnp.where(has_next, halo_recv[1], 0.0)
    first = jnp.where(left_wide, from_prev, pltpu.roll(from_next, halo, 1))
    second = jnp.where(left_wide, pltpu.roll(from_prev, halo, 1), from_next)
    x_all[0 : 2 * levels, cells:] = first
    x_all[2 * levels : 3 * levels, cells:] = second[:levels]
    x_all[3 * levels :, cells:] = second[levels:] + above_halo
    mont = x_all[3 * levels :, 0:cells] + above_row
    x_all[3 * levels :, 0:cells] = mont
    x_high, x_low = split(x_all[...])
    x_split[0 : 4 * levels, :] = x_high
    x_split[4 * levels :, :] = x_low

    temp_sum = jnp.zeros((levels, cells), F32)
    salt_sum = jnp.zeros((levels, cells), F32)
    rate_sum = jnp.zeros((levels, cells), F32)
    for e in range(edges):
        g = jnp.dot(x_split[...], hot[e], preferred_element_type=F32)
        g = g[: 4 * levels] + g[4 * levels :]
        weight = jnp.where(near_ref[e : e + 1, :] < blank_slot, ew_ref[e : e + 1, :], 0.0)
        step = g[3 * levels :] - mont
        flow = weight * step
        mixed = flow + weight * (2.0 * mixing)
        temp_sum = temp_sum + mixed * (g[:levels] - tr_ref[0])
        salt_sum = salt_sum + mixed * (g[levels : 2 * levels] - tr_ref[1])
        rate_sum = rate_sum + flow * (g[2 * levels : 3 * levels] + th_ref[...])
    temp_new = tr_ref[0] + (0.5 * time_step) * temp_sum
    salt_new = tr_ref[1] + (0.5 * time_step) * salt_sum
    prov = th_ref[...] + (0.5 * time_step) * rate_sum
    tr_out[0] = temp_new
    tr_out[1] = salt_new
    prov_ref[...] = prov
    put_rows(col_mine, 0, jnp.sum(prov, axis=0, keepdims=True))
    put_rows(col_mine, 4, jnp.sum(prov * temp_new, axis=0, keepdims=True))
    put_rows(col_mine, 8, jnp.sum(prov * salt_new, axis=0, keepdims=True))
    put_rows(col_mine, 12, jnp.sum(temp_new, axis=0, keepdims=True))
    put_rows(col_mine, 16, jnp.sum(salt_new, axis=0, keepdims=True))
    col_mine[20:24, :] = jnp.zeros((4, LANES), F32)
    col_copy = pltpu.make_async_remote_copy(
        src_ref=col_mine,
        dst_ref=col_other,
        send_sem=col_ss,
        recv_sem=col_rs,
        device_id=at(q, 1 - lev),
        device_id_type=pl.DeviceIdType.MESH,
    )
    col_copy.start()

    phis, heights, forcings = [], [], []
    for s in range(window):
        height, phi = pair(state_all[0, s, 0:8, :])
        zero_part, zero_total = pair(state_all[0, s, 8:16, :])
        one_part = pair(state_all[1, s, 8:16, :])[0]
        one_thick = pair(state_all[1, s, 16:24, :])[0]
        forcings.append((zero_part + one_part + zero_total * one_thick) / full_levels)
        phis.append(phi)
        heights.append(height)

    def subcycle(step_index, state):
        phis, heights = state
        phis = [p - fast_step * (h + f) for p, h, f in zip(phis, heights, forcings)]
        listed = []
        for s in range(window):
            got = take_listed(phis[s], list_of(s))
            ok = slot_exists(s)
            listed.append(got if ok is True else jnp.where(ok, got, 0.0))
        none = jnp.zeros((1, LANES), F32)
        out = []
        for s in range(window):
            before = listed[s - 1] if s > 0 else none
            after = listed[s + 1] if s < window - 1 else none
            rim = jnp.where(left8[0:1], before, after)
            sources = [
                jnp.broadcast_to(phis[s][c : c + 1, :], (8, LANES)) for c in range(chunks)
            ] + [jnp.broadcast_to(rim, (8, LANES))]
            total = jnp.zeros((8, LANES), F32)
            for j in range(edges // 2):
                index = table_all[s, 8 * j : 8 * j + 8, :].astype(jnp.int32)
                weight = table_all[s, 4 * edges + 8 * j : 4 * edges + 8 * j + 8, :]
                low = jnp.bitwise_and(index, LANES - 1)
                high = jnp.right_shift(index, 7)
                near = jnp.zeros((8, LANES), F32)
                for c, source in enumerate(sources):
                    near = jnp.where(high == c, lanes_of(source, low), near)
                total = total + weight * (near - phis[s])
            total = total + pltpu.roll(total, 4, 0)
            out.append(heights[s] + fast_step * total)
        return phis, out

    phis, heights = lax.fori_loop(0, SUBCYCLES, subcycle, (phis, heights))
    if whole:
        phi_end, ssh_end = phis[0], heights[0]
        for s in range(1, window):
            phi_end = jnp.where(q == s, phis[s], phi_end)
            ssh_end = jnp.where(q == s, heights[s], ssh_end)
    else:
        phi_end, ssh_end = phis[reach], heights[reach]
    ssh_out[...] = ssh_end[0:4, :]

    col_copy.wait_recv()
    column, heat = pair(col_mine[0:8, :] + col_other[0:8, :])
    salt_col, heat_plain = pair(col_mine[8:16, :] + col_other[8:16, :])
    salt_plain = pair(col_mine[16:24, :] + col_other[16:24, :])[0]
    correction = (full_levels + ssh_end - column) / full_levels
    surface = [
        ssh_end,
        phi_end,
        (heat + correction * heat_plain) / full_levels,
        (salt_col + correction * salt_plain) / full_levels,
    ]

    source = src_ref[...]
    low = jnp.bitwise_and(source, LANES - 1)
    high = jnp.right_shift(source, 7)
    contrib = []
    for f in range(4):
        got = jnp.zeros((8, LANES), F32)
        for c in range(chunks):
            row = jnp.broadcast_to(surface[f][c : c + 1, :], (8, LANES))
            got = jnp.where(high == c, lanes_of(row, low), got)
        value = got * rw_ref[...]
        top = value.astype(BF16).astype(F32)
        contrib.append((top, value - top))
    keys = own_ref[...] * 4 + jnp.right_shift(loc_ref[...], 7)
    parts = []
    for k in range(entry_rows):
        pieces = []
        for half in range(2):
            for f in (0, 2):
                one = jnp.broadcast_to(contrib[f][half][k : k + 1, :], (8, LANES))
                two = jnp.broadcast_to(contrib[f + 1][half][k : k + 1, :], (8, LANES))
                pieces.append(jnp.where(upper, one, two))
        parts.append(pieces)

    def fill(p):
        start = p * 16 if isinstance(p, int) else pl.multiple_of(p * 16, 16)
        start_low = start + members * 16
        if not isinstance(p, int):
            start_low = pl.multiple_of(start_low, 16)
        for k in range(entry_rows):
            hit = jnp.broadcast_to(keys[k : k + 1, :], (8, LANES)) == chunk8 + p * 4
            a, b, c, d = [jnp.where(hit, piece, 0.0) for piece in parts[k]]
            lanes = pl.ds(k * LANES, LANES)
            flux_lhs[pl.ds(start, 16), lanes] = jnp.concatenate([a, b], axis=0).astype(BF16)
            flux_lhs[pl.ds(start_low, 16), lanes] = jnp.concatenate([c, d], axis=0).astype(BF16)

    repeat(members, fill)
    block = lax.dot_general(
        flux_lhs[...],
        flux_hot[...],
        (((1,), (1,)), ((), ())),
        preferred_element_type=F32,
    )
    flux_send[...] = (block[: members * 16] + block[members * 16 :]).reshape(members, 16, LANES)

    def flux_copy(i):
        p = lax.rem(q + 1 + i, members)
        return pltpu.make_async_remote_copy(
            src_ref=flux_send.at[p],
            dst_ref=flux_recv.at[q],
            send_sem=flux_ss.at[i],
            recv_sem=flux_rs.at[q],
            device_id=at(p, lev),
            device_id_type=pl.DeviceIdType.MESH,
        )

    repeat(members - 1, lambda i: flux_copy(i).start())
    for c in range(chunks):
        part = slice(c * LANES, (c + 1) * LANES)
        th_out[:, part] = prov_ref[:, part] + correction[c : c + 1, :]

    def flux_arrived(i):
        p = lax.rem(q + 1 + i, members)
        pltpu.make_async_remote_copy(
            src_ref=flux_send.at[p],
            dst_ref=flux_recv.at[p],
            send_sem=flux_ss.at[i],
            recv_sem=flux_rs.at[p],
            device_id=at(p, lev),
            device_id_type=pl.DeviceIdType.MESH,
        ).wait_recv()

    flux_recv[q] = flux_send[q]
    repeat(members - 1, flux_arrived)
    total = jnp.sum(flux_recv[...], axis=0)
    for f in range(4):
        for c in range(chunks):
            atm_out[f : f + 1, c * LANES : (c + 1) * LANES] = total[f * 4 + c : f * 4 + c + 1, :]

    pl.when(has_prev)(lambda: halo_copy(0, prev_q).wait_send())
    pl.when(has_next)(lambda: halo_copy(1, next_q).wait_send())
    for copy, ok in sends:
        guarded(ok, copy.wait_send)
    col_copy.wait_send()
    repeat(members - 1, lambda i: flux_copy(i).wait_send())


def per_device(
    n_cells,
    n_sub,
    tracers,
    thickness,
    ssh,
    potential,
    neighbours,
    edge_weight,
    send_list,
    remap_src,
    remap_owner,
    remap_local,
    remap_weight,
):
    members = n_cells * n_sub
    levels, cells = thickness.shape
    halo = send_list.shape[1]
    edges = neighbours.shape[0]
    entries = remap_src.shape[0]
    reach = SUBCYCLES
    window = members if members <= 2 * reach + 1 else 2 * reach + 1
    rows = entries // LANES
    table_rows = 8 * edges + 8
    wide = cells + 2 * halo
    dma = pltpu.SemaphoreType.DMA
    kernel = functools.partial(ocean_kernel, n_cells, n_sub, reach, window)
    vmem = pl.BlockSpec(memory_space=pltpu.VMEM)
    tr, th, ssh_new, atm = pl.pallas_call(
        kernel,
        out_shape=(
            jax.ShapeDtypeStruct(tracers.shape, F32),
            jax.ShapeDtypeStruct(thickness.shape, F32),
            jax.ShapeDtypeStruct((cells // LANES, LANES), F32),
            jax.ShapeDtypeStruct((4, cells), F32),
        ),
        in_specs=[vmem] * 11,
        out_specs=(vmem,) * 4,
        scratch_shapes=[
            pltpu.VMEM((2, 2 * levels, LANES), F32),
            pltpu.VMEM((2, 2 * levels, LANES), F32),
            pltpu.VMEM((window, table_rows, LANES), F32),
            pltpu.VMEM((24, LANES), F32),
            pltpu.VMEM((2, window, 24, LANES), F32),
            pltpu.VMEM((24, LANES), F32),
            pltpu.VMEM((24, LANES), F32),
            pltpu.VMEM((members, 16, LANES), F32),
            pltpu.VMEM((members, 16, LANES), F32),
            pltpu.VMEM((4 * levels, wide), F32),
            pltpu.VMEM((8 * levels, wide), BF16),
            pltpu.VMEM((edges, wide, cells), BF16),
            pltpu.VMEM((levels, cells), F32),
            pltpu.VMEM((2 * members * 16, entries), BF16),
            pltpu.VMEM((LANES, entries), BF16),
            dma((2,)),
            dma((2,)),
            dma((window,)),
            dma((window,)),
            dma((2, window)),
            dma((2, window)),
            dma,
            dma,
            dma((members,)),
            dma((members,)),
        ],
        compiler_params=pltpu.CompilerParams(
            collective_id=0, has_side_effects=True, vmem_limit_bytes=48 * 1024 * 1024
        ),
        cost_estimate=pl.CostEstimate(
            flops=2 * 8 * levels * wide * cells * edges,
            bytes_accessed=8 * levels * cells * 4,
            transcendentals=0,
        ),
    )(
        tracers,
        thickness,
        ssh.reshape(-1, LANES),
        potential.reshape(-1, LANES),
        neighbours,
        edge_weight,
        jnp.concatenate([send_list[1:2], send_list[0:1]], axis=1),
        remap_src.reshape(rows, LANES),
        remap_owner.reshape(rows, LANES),
        remap_local.reshape(rows, LANES),
        remap_weight.reshape(rows, LANES),
    )
    return tr, th, ssh_new.reshape(cells), atm


def solution(mesh):
    placed = (
        P(None, "lev", ("groups", "cells", "sub")),
        P("lev", ("groups", "cells", "sub")),
        P(("groups", "cells", "sub")),
        P(("groups", "cells", "sub")),
        P(None, ("cells", "sub")),
        P(None, ("cells", "sub")),
        P(None, ("cells", "sub")),
        P(("cells", "sub")),
        P(("cells", "sub"), None),
        P(("cells", "sub")),
        P(("cells", "sub")),
    )
    return jax.shard_map(
        functools.partial(per_device, mesh.shape["cells"], mesh.shape["sub"]),
        mesh=mesh,
        in_specs=placed,
        out_specs=(
            P(None, "lev", ("groups", "cells", "sub")),
            P("lev", ("groups", "cells", "sub")),
            P(("groups", "cells", "sub")),
            P(None, ("groups", "cells", "sub")),
        ),
        check_vma=False,
    )
```

time: 237 us -> 39.2 us (0.17)
  waiting for transfers between devices: 90.7 us -> 0 us
  starting transfers between devices: 74.8 us -> 0 us
  Pallas kernels: 0 us -> 28.2 us
  matrix products: 19 us -> 0 us
  other arithmetic: 16.2 us -> 0.07 us
  between operations: 14.5 us -> 0.66 us
  local copies, waits for them, and re-layouts: 15.8 us -> 9.79 us
  blocking collectives: 5.22 us -> 0 us
    ppermute x22 -> x0, starting transfers between devices: 74.8 us -> none  [the longest x11 60.5 us: extended_2(): lax.ppermute(lax.slice_in_dim(block, block.shape[dim] - width, None, axis...]
    reduce_scatter x1 -> x0, waiting for transfers between devices: 73.3 us -> none  [per_device(): lax.psum_scatter(dense_flux, ('cells', 'sub'), scatter_dimension=1, tiled...]
    pallas_call x0 -> x1, Pallas kernels: none -> 28.2 us  [per_device(): pl.pallas_call(kernel, out_shape=(jax.ShapeDtypeStruct(tracers.shape, F32...]
    dot_general x20 -> x0, matrix products: 19 us -> none  [the longest x10 16.5 us: subcycle(): jnp.dot(padded, spread_table, precision=lax.Precision.HIGHEST)]
    ppermute x22 -> x0, waiting for transfers between devices: 17.3 us -> none  [the longest x11 12.7 us: extended_2(): lax.ppermute(lax.slice_in_dim(block, block.shape[dim] - width, None, axis...]
    gather x16 -> x0, local copies, waits for them, and re-layouts: 11.9 us -> none  [the longest x12 10.5 us: stencil(): gathered = extended[:, near_index]]
    scatter-add x1 -> x0, other arithmetic: 10.7 us -> none  [per_device(): dense_flux = jnp.zeros((surface.shape[0], members * ATM_DEV), jnp.float32...]
    unnamed x27 -> x24, local copies, waits for them, and re-layouts: 2.43 us -> 9.03 us
  transfers between devices with their start and end apart: 23 -> 0, of which waited for: 12 -> 0; matrix products, arithmetic and copies ran while one was open for 1% -> 0% of each run, Pallas kernels for 0% -> 0%
where the time goes in v1:
time: 39.2 us; the launch traced here: 38.7 us
  Pallas kernels  28.2 us (72%)
  local copies, waits for them, and re-layouts  9.79 us (25%)
  between operations  0.66 us (2%)
    pallas_call x1, Pallas kernels, per_device(): pl.pallas_call(kernel, out_shape=(jax.ShapeDtypeStruct(tracers.shape, F32...  28.2 us
    unnamed x24, local copies, waits for them, and re-layouts  9.03 us

profile of v1, /device:TPU:0, one launch (start us, length us, event | category | flops | bytes accessed | tf_op | source)
XLA Modules:
  0.0 38.7 jit_solution(11420148333176454276)
XLA Ops:
  0.6 0.0 copy-start.2
  0.6 0.8 %fusion = (s32[1,64]{1,0:T(1,128)S(1)}, s32[1,64]{1,0:T(1,128)S(1)}) fusion(s32[2,64]{1,0:T(2,128)} %param.17), kind=kLoop, calls=%fused_computation.1 | loop fusion | bytes 1024 | tf_op jit(solution)/shard_map/slice | solution.py:651
  1.4 0.0 copy-start.8
  1.4 0.1 pad_add_fusion.send_ref
  1.5 0.0 copy-done.2
  1.5 0.6 %copy-done.8 = f32[512]{0:T(512)S(1)} copy-done((f32[512]{0:T(512)S(1)}, f32[512]{0:T(512)}, u32[]{:S(2)}) %copy-start.8) | copy-done | bytes 2072
  2.1 0.0 copy-start
  2.1 0.9 %copy-done = f32[2,40,512]{2,1,0:T(8,128)S(1)} copy-done((f32[2,40,512]{2,1,0:T(8,128)S(1)}, f32[2,40,512]{2,1,0:T(8,128)}, u32[]{:S(2)}) %copy-start) | copy-done | bytes 163864
  3.0 0.0 copy-start.1
  3.0 0.9 %copy-done.1 = f32[40,512]{1,0:T(8,128)S(1)} copy-done((f32[40,512]{1,0:T(8,128)S(1)}, f32[40,512]{1,0:T(8,128)}, u32[]{:S(2)}) %copy-start.1) | copy-done | bytes 81944
  3.9 0.0 copy-start.3
  3.9 0.7 %copy-done.3 = f32[6,512]{1,0:T(8,128)S(1)} copy-done((f32[6,512]{1,0:T(8,128)S(1)}, f32[6,512]{1,0:T(8,128)}, u32[]{:S(2)}) %copy-start.3) | copy-done | bytes 12312
  4.6 0.0 copy-start.4
  4.6 0.7 %copy-done.4 = s32[1024]{0:T(1024)S(1)} copy-done((s32[1024]{0:T(1024)S(1)}, s32[1024]{0:T(1024)}, u32[]{:S(2)}) %copy-start.4) | copy-done | bytes 4120
  5.3 0.0 copy-start.5
  5.3 0.7 %copy-done.5 = s32[1024,1]{0,1:T(1,128)S(1)} copy-done((s32[1024,1]{0,1:T(1,128)S(1)}, s32[1024,1]{0,1:T(1,128)}, u32[]{:S(2)}) %copy-start.5) | copy-done | bytes 4120
  6.0 0.7 %copy-done.6 = s32[1024]{0:T(1024)S(1)} copy-done((s32[1024]{0:T(1024)S(1)}, s32[1024]{0:T(1024)}, u32[]{:S(2)}) %copy-start.6) | copy-done | bytes 4120
  6.7 0.7 %copy-done.7 = f32[1024]{0:T(1024)S(1)} copy-done((f32[1024]{0:T(1024)S(1)}, f32[1024]{0:T(1024)}, u32[]{:S(2)}) %copy-start.7) | copy-done | bytes 4120
  7.4 0.7 %copy-done.9 = f32[512]{0:T(512)S(1)} copy-done((f32[512]{0:T(512)S(1)}, f32[512]{0:T(512)}, u32[]{:S(2)}) %copy-start.9) | copy-done | bytes 2072
  8.0 28.2 %shard_map.138 = (f32[2,40,512]{2,1,0:T(8,128)S(1)}, f32[40,512]{1,0:T(8,128)S(1)}, f32[4,128]{1,0:T(4,128)S(1)}, f32[4,512]{1,0:T(4,128)S(1)}) custom-call(f32[2,40,512]{2,1,0:T(8,128)S(1)} %copy-done, f32[40,512]{1,0:T(8,128)S(1)} %copy-done.1, f32[4,128]{1,0:T(4,128)S(1)} %bitcast.12, f32[4,128]{1,0:T(4,128)S(1)} %bitcast.13, s32[6,512]{1,0:T(8,128)S(1)} %copy-done.2, ...), custom_call_target="tpu_custom_call" | custom-call | flops 1258291200 | bytes 655360 | tf_op jit(solution)/shard_map/pallas_call | solution.py:599
  36.2 0.7 %copy.19 = f32[2,40,512]{2,1,0:T(8,128)} copy(f32[2,40,512]{2,1,0:T(8,128)S(1)} %get-tuple-element.18) | data formatting | bytes 327680
  36.9 0.6 %copy.20 = f32[40,512]{1,0:T(8,128)} copy(f32[40,512]{1,0:T(8,128)S(1)} %get-tuple-element.19) | data formatting | bytes 163840
  37.5 0.6 %copy.21 = f32[512]{0:T(512)} copy(f32[512]{0:T(512)S(1)} %bitcast.7) | data formatting | bytes 4096
  38.1 0.6 %copy.22 = f32[4,512]{1,0:T(4,128)} copy(f32[4,512]{1,0:T(4,128)S(1)} %get-tuple-element.21) | data formatting | bytes 16384
  (3 shorter events, 0.0 us)
Async XLA Ops:
  0.6 0.8 %copy-start.2 = (s32[6,512]{1,0:T(8,128)S(1)}, s32[6,512]{1,0:T(8,128)}, u32[]{:S(2)}) copy-start(s32[6,512]{1,0:T(8,128)} %near_ref.1) | copy-start | bytes 36868
  1.4 0.7 %copy-start.8 = (f32[512]{0:T(512)S(1)}, f32[512]{0:T(512)}, u32[]{:S(2)}) copy-start(f32[512]{0:T(512)} %param.13) | copy-start | bytes 6148
  2.1 0.9 %copy-start = (f32[2,40,512]{2,1,0:T(8,128)S(1)}, f32[2,40,512]{2,1,0:T(8,128)}, u32[]{:S(2)}) copy-start(f32[2,40,512]{2,1,0:T(8,128)} %tr_ref.1) | copy-start | bytes 491524
  3.0 0.9 %copy-start.1 = (f32[40,512]{1,0:T(8,128)S(1)}, f32[40,512]{1,0:T(8,128)}, u32[]{:S(2)}) copy-start(f32[40,512]{1,0:T(8,128)} %th_ref.1) | copy-start | bytes 245764
  3.9 0.7 %copy-start.3 = (f32[6,512]{1,0:T(8,128)S(1)}, f32[6,512]{1,0:T(8,128)}, u32[]{:S(2)}) copy-start(f32[6,512]{1,0:T(8,128)} %ew_ref.1) | copy-start | bytes 36868
  4.6 0.7 %copy-start.4 = (s32[1024]{0:T(1024)S(1)}, s32[1024]{0:T(1024)}, u32[]{:S(2)}) copy-start(s32[1024]{0:T(1024)} %param.18) | copy-start | bytes 12292
  5.3 0.7 %copy-start.5 = (s32[1024,1]{0,1:T(1,128)S(1)}, s32[1024,1]{0,1:T(1,128)}, u32[]{:S(2)}) copy-start(s32[1024,1]{0,1:T(1,128)} %param.19) | copy-start | bytes 12292
  6.0 0.7 %copy-start.6 = (s32[1024]{0:T(1024)S(1)}, s32[1024]{0:T(1024)}, u32[]{:S(2)}) copy-start(s32[1024]{0:T(1024)} %param.20) | copy-start | bytes 12292
  6.7 0.7 %copy-start.7 = (f32[1024]{0:T(1024)S(1)}, f32[1024]{0:T(1024)}, u32[]{:S(2)}) copy-start(f32[1024]{0:T(1024)} %param.21) | copy-start | bytes 12292
  7.4 0.7 %copy-start.9 = (f32[512]{0:T(512)S(1)}, f32[512]{0:T(512)}, u32[]{:S(2)}) copy-start(f32[512]{0:T(512)} %param.14) | copy-start | bytes 6148

commit v2 on v1

--- a/solution.py
+++ b/solution.py
@@ -54,21 +54,21 @@
     n_sub,
     reach,
     window,
-    tr_ref,
-    th_ref,
-    ssh_ref,
-    pot_ref,
-    near_ref,
-    ew_ref,
-    send_ref,
-    src_ref,
-    own_ref,
-    loc_ref,
-    rw_ref,
-    tr_out,
-    th_out,
-    ssh_out,
-    atm_out,
+    tr_in,
+    th_in,
+    ssh_in,
+    pot_in,
+    near_in,
+    ew_in,
+    list_in,
+    src_in,
+    own_in,
+    loc_in,
+    rw_in,
+    tr_res,
+    th_res,
+    ssh_res,
+    atm_res,
     halo_send,
     halo_recv,
     table_all,
@@ -84,6 +84,23 @@
     prov_ref,
     flux_lhs,
     flux_hot,
+    tr_ref,
+    th_ref,
+    ssh_ref,
+    pot_ref,
+    near_ref,
+    ew_ref,
+    list_ref,
+    src_ref,
+    own_ref,
+    loc_ref,
+    rw_ref,
+    in_sem,
+    tr_out,
+    th_out,
+    ssh_out,
+    atm_out,
+    out_sem,
     halo_ss,
     halo_rs,
     table_ss,
@@ -99,7 +116,7 @@
     levels, cells = th_ref.shape
     edges = near_ref.shape[0]
     chunks = cells // LANES
-    halo = send_ref.shape[1] // 2
+    halo = list_ref.shape[1]
     full_levels = 2 * levels
     q = lax.axis_index("cells") * n_sub + lax.axis_index("sub")
     lev = lax.axis_index("lev")
@@ -123,6 +140,34 @@
 
     same = range(1, members) if whole else [i for i in range(window) if i != reach]
     both = range(window)
+
+    loads = [
+        pltpu.make_async_copy(a, b, in_sem.at[i])
+        for i, (a, b) in enumerate(
+            (
+                (tr_in, tr_ref),
+                (th_in, th_ref),
+                (ssh_in, ssh_ref),
+                (pot_in, pot_ref),
+                (near_in, near_ref),
+                (ew_in, ew_ref),
+                (list_in, list_ref),
+                (src_in, src_ref),
+                (own_in, own_ref),
+                (loc_in, loc_ref),
+                (rw_in, rw_ref),
+            )
+        )
+    ]
+    for copy in loads:
+        copy.start()
+
+    results = [
+        pltpu.make_async_copy(a, b, out_sem.at[i])
+        for i, (a, b) in enumerate(
+            ((tr_out, tr_res), (th_out, th_res), (ssh_out, ssh_res), (atm_out, atm_res))
+        )
+    ]
 
     barrier = pltpu.get_barrier_semaphore()
 
@@ -165,6 +210,10 @@
     def put_rows(ref, start, row):
         for c in range(chunks):
             ref[start + c : start + c + 1, :] = row[:, c * LANES : (c + 1) * LANES]
+
+    for copy in loads:
+        copy.wait()
+    listed_row = jnp.concatenate([list_ref[1:2, :], list_ref[0:1, :]], axis=1)
 
     temp = tr_ref[0]
     salt = tr_ref[1]
@@ -192,7 +241,7 @@
     put_rows(state_mine, 8, jnp.sum(thick * part_mont, axis=0, keepdims=True))
     put_rows(state_mine, 12, jnp.sum(load, axis=0, keepdims=True))
     put_rows(state_mine, 16, jnp.sum(thick, axis=0, keepdims=True))
-    state_mine[20:24, :] = jnp.zeros((4, LANES), F32)
+    state_mine[20:24, :] = jnp.broadcast_to(listed_row.astype(F32), (4, LANES))
 
     my_table = table_all.at[mine]
     blank_slot = cells + 2 * halo
@@ -201,14 +250,11 @@
         weight = jnp.where(index_row < blank_slot, ew_ref[e : e + 1, :], 0.0)
         put_rows(my_table, e * 4, index_row.astype(F32))
         put_rows(my_table, edges * 4 + e * 4, weight)
-    my_table[8 * edges : 8 * edges + 8, :] = jnp.broadcast_to(
-        send_ref[...].astype(F32), (8, LANES)
-    )
 
     pick = (
         (
             lax.broadcasted_iota(jnp.int32, (cells, LANES), 0)
-            == jnp.broadcast_to(send_ref[...], (cells, LANES))
+            == jnp.broadcast_to(listed_row, (cells, LANES))
         )
         .astype(F32)
         .astype(BF16)
@@ -354,11 +400,10 @@
         keep = s != mine
         guarded(keep if ok is True else keep & ok, body)
 
-    for s in range(window):
-        wait_table(s)
-
     def list_of(slot):
-        return table_all[slot, 8 * edges : 8 * edges + 8, :].astype(jnp.int32)
+        return jnp.broadcast_to(
+            state_all[0, slot, 20:21, :].astype(jnp.int32), (8, LANES)
+        )
 
     above_mine = jnp.where(lower_level, total_of(mine), 0.0)
     above_row = jnp.concatenate([above_mine[c : c + 1, :] for c in range(chunks)], axis=1)
@@ -418,6 +463,10 @@
         device_id_type=pl.DeviceIdType.MESH,
     )
     col_copy.start()
+    results[0].start()
+
+    for s in range(window):
+        wait_table(s)
 
     phis, heights, forcings = [], [], []
     for s in range(window):
@@ -469,6 +518,7 @@
     else:
         phi_end, ssh_end = phis[reach], heights[reach]
     ssh_out[...] = ssh_end[0:4, :]
+    results[2].start()
 
     col_copy.wait_recv()
     column, heat = pair(col_mine[0:8, :] + col_other[0:8, :])
@@ -542,6 +592,8 @@
         part = slice(c * LANES, (c + 1) * LANES)
         th_out[:, part] = prov_ref[:, part] + correction[c : c + 1, :]
 
+    results[1].start()
+
     def flux_arrived(i):
         p = lax.rem(q + 1 + i, members)
         pltpu.make_async_remote_copy(
@@ -560,12 +612,27 @@
         for c in range(chunks):
             atm_out[f : f + 1, c * LANES : (c + 1) * LANES] = total[f * 4 + c : f * 4 + c + 1, :]
 
+    results[3].start()
+
     pl.when(has_prev)(lambda: halo_copy(0, prev_q).wait_send())
     pl.when(has_next)(lambda: halo_copy(1, next_q).wait_send())
     for copy, ok in sends:
         guarded(ok, copy.wait_send)
     col_copy.wait_send()
     repeat(members - 1, lambda i: flux_copy(i).wait_send())
+    for copy in results:
+        copy.wait()
+
+
+def write_out(*refs):
+    sems = refs[-1]
+    copies = [
+        pltpu.make_async_copy(refs[i], refs[4 + i], sems.at[i]) for i in range(4)
+    ]
+    for copy in copies:
+        copy.start()
+    for copy in copies:
+        copy.wait()
 
 
 def per_device(
@@ -591,11 +658,11 @@
     reach = SUBCYCLES
     window = members if members <= 2 * reach + 1 else 2 * reach + 1
     rows = entries // LANES
-    table_rows = 8 * edges + 8
+    table_rows = 8 * edges
     wide = cells + 2 * halo
     dma = pltpu.SemaphoreType.DMA
     kernel = functools.partial(ocean_kernel, n_cells, n_sub, reach, window)
-    vmem = pl.BlockSpec(memory_space=pltpu.VMEM)
+    hbm = pl.BlockSpec(memory_space=pltpu.HBM)
     tr, th, ssh_new, atm = pl.pallas_call(
         kernel,
         out_shape=(
@@ -604,8 +671,8 @@
             jax.ShapeDtypeStruct((cells // LANES, LANES), F32),
             jax.ShapeDtypeStruct((4, cells), F32),
         ),
-        in_specs=[vmem] * 11,
-        out_specs=(vmem,) * 4,
+        in_specs=[hbm] * 11,
+        out_specs=(hbm,) * 4,
         scratch_shapes=[
             pltpu.VMEM((2, 2 * levels, LANES), F32),
             pltpu.VMEM((2, 2 * levels, LANES), F32),
@@ -622,6 +689,23 @@
             pltpu.VMEM((levels, cells), F32),
             pltpu.VMEM((2 * members * 16, entries), BF16),
             pltpu.VMEM((LANES, entries), BF16),
+            pltpu.VMEM(tracers.shape, F32),
+            pltpu.VMEM(thickness.shape, F32),
+            pltpu.VMEM((cells // LANES, LANES), F32),
+            pltpu.VMEM((cells // LANES, LANES), F32),
+            pltpu.VMEM(neighbours.shape, jnp.int32),
+            pltpu.VMEM(neighbours.shape, F32),
+            pltpu.VMEM(send_list.shape, jnp.int32),
+            pltpu.VMEM((rows, LANES), jnp.int32),
+            pltpu.VMEM((rows, LANES), jnp.int32),
+            pltpu.VMEM((rows, LANES), jnp.int32),
+            pltpu.VMEM((rows, LANES), F32),
+            dma((11,)),
+            pltpu.VMEM(tracers.shape, F32),
+            pltpu.VMEM(thickness.shape, F32),
+            pltpu.VMEM((cells // LANES, LANES), F32),
+            pltpu.VMEM((4, cells), F32),
+            dma((4,)),
             dma((2,)),
             dma((2,)),
             dma((window,)),
@@ -634,7 +718,7 @@
             dma((members,)),
         ],
         compiler_params=pltpu.CompilerParams(
-            collective_id=0, has_side_effects=True, vmem_limit_bytes=48 * 1024 * 1024
+            collective_id=0, has_side_effects=True, vmem_limit_bytes=60 * 1024 * 1024
         ),
         cost_estimate=pl.CostEstimate(
             flops=2 * 8 * levels * wide * cells * edges,
@@ -648,12 +732,20 @@
         potential.reshape(-1, LANES),
         neighbours,
         edge_weight,
-        jnp.concatenate([send_list[1:2], send_list[0:1]], axis=1),
+        send_list,
         remap_src.reshape(rows, LANES),
         remap_owner.reshape(rows, LANES),
         remap_local.reshape(rows, LANES),
         remap_weight.reshape(rows, LANES),
     )
+    tr, th, ssh_new, atm = pl.pallas_call(
+        write_out,
+        out_shape=tuple(jax.ShapeDtypeStruct(a.shape, F32) for a in (tr, th, ssh_new, atm)),
+        in_specs=[hbm] * 4,
+        out_specs=(hbm,) * 4,
+        scratch_shapes=[dma((4,))],
+        compiler_params=pltpu.CompilerParams(vmem_limit_bytes=60 * 1024 * 1024),
+    )(tr, th, ssh_new, atm)
     return tr, th, ssh_new.reshape(cells), atm
 
 

time: 39.2 us -> 36.1 us (0.921)
  local copies, waits for them, and re-layouts: 9.79 us -> 0 us
  Pallas kernels: 28.2 us -> 35.3 us
    unnamed x24 -> x0, local copies, waits for them, and re-layouts: 9.03 us -> none
    pallas_call x0 -> x1, Pallas kernels: none -> 8.89 us  [per_device(): pl.pallas_call(write_out, out_shape=tuple((jax.ShapeDtypeStruct(a.shape,...]
    pallas_call x1, Pallas kernels: 28.2 us -> 26.4 us  [per_device(): pl.pallas_call(kernel, out_shape=(jax.ShapeDtypeStruct(tracers.shape, F32...]
    slice x1 -> x0, local copies, waits for them, and re-layouts: 0.76 us -> none  [per_device(): send_list[1:2]]
where the time goes in v2:
time: 36.1 us; the launch traced here: 35.9 us
  Pallas kernels  35.3 us (98%)
  between operations  0.64 us (2%)
    pallas_call x1, Pallas kernels, per_device(): pl.pallas_call(kernel, out_shape=(jax.ShapeDtypeStruct(tracers.shape, F32...  26.4 us
    pallas_call x1, Pallas kernels, per_device(): pl.pallas_call(write_out, out_shape=tuple((jax.ShapeDtypeStruct(a.shape,...  8.89 us

profile of v2, /device:TPU:0, one launch (start us, length us, event | category | flops | bytes accessed | tf_op | source)
XLA Modules:
  0.0 35.9 jit_solution(11368361379774611459)
XLA Ops:
  0.6 26.4 %shard_map.138 = (f32[2,40,512]{2,1,0:T(8,128)}, f32[40,512]{1,0:T(8,128)}, f32[4,128]{1,0:T(4,128)}, f32[4,512]{1,0:T(4,128)}) custom-call(f32[2,40,512]{2,1,0:T(8,128)} %tr_in.1, f32[40,512]{1,0:T(8,128)} %th_in.1, f32[4,128]{1,0:T(4,128)} %bitcast.11, f32[4,128]{1,0:T(4,128)} %bitcast.12, s32[6,512]{1,0:T(8,128)} %near_in.1, f32[6,512]{1,0:T(8,128)} %ew_in.1, ...), custom_call_target="tpu_custom_call" | custom-call | flops 1258291200 | bytes 655360 | tf_op jit(solution)/shard_map/pallas_call | solution.py:666
  27.0 8.9 %shard_map.139 = (f32[2,40,512]{2,1,0:T(8,128)}, f32[40,512]{1,0:T(8,128)}, f32[4,128]{1,0:T(4,128)}, f32[4,512]{1,0:T(4,128)}) custom-call(f32[2,40,512]{2,1,0:T(8,128)} %get-tuple-element.12.refs_0_, f32[40,512]{1,0:T(8,128)} %get-tuple-element.13.refs_1_, f32[4,128]{1,0:T(4,128)} %get-tuple-element.14.refs_2_, f32[4,512]{1,0:T(4,128)} %get-tuple-element.15.refs_3_), custom_call_target="tpu_custom_call" | custom-call | tf_op jit(solution)/shard_map/pallas_call | solution.py:741

commit v3 on v2

--- a/solution.py
+++ b/solution.py
@@ -625,13 +625,15 @@
 
 
 def write_out(*refs):
-    sems = refs[-1]
-    copies = [
-        pltpu.make_async_copy(refs[i], refs[4 + i], sems.at[i]) for i in range(4)
-    ]
-    for copy in copies:
+    in_sem, out_sem = refs[12:]
+    fetch = [pltpu.make_async_copy(refs[i], refs[8 + i], in_sem.at[i]) for i in range(4)]
+    store = [pltpu.make_async_copy(refs[8 + i], refs[4 + i], out_sem.at[i]) for i in range(4)]
+    for copy in fetch:
         copy.start()
-    for copy in copies:
+    for i in range(4):
+        fetch[i].wait()
+        store[i].start()
+    for copy in store:
         copy.wait()
 
 
@@ -743,7 +745,8 @@
         out_shape=tuple(jax.ShapeDtypeStruct(a.shape, F32) for a in (tr, th, ssh_new, atm)),
         in_specs=[hbm] * 4,
         out_specs=(hbm,) * 4,
-        scratch_shapes=[dma((4,))],
+        scratch_shapes=[pltpu.VMEM(a.shape, F32) for a in (tr, th, ssh_new, atm)]
+        + [dma((4,)), dma((4,))],
         compiler_params=pltpu.CompilerParams(vmem_limit_bytes=60 * 1024 * 1024),
     )(tr, th, ssh_new, atm)
     return tr, th, ssh_new.reshape(cells), atm

time: 36.1 us -> 28.9 us (0.80)
  Pallas kernels: 35.3 us -> 28.1 us
    pallas_call x1, Pallas kernels: 8.89 us -> 1.68 us  [per_device(): pl.pallas_call(write_out, out_shape=tuple((jax.ShapeDtypeStruct(a.shape,...]
where the time goes in v3:
time: 28.9 us; the launch traced here: 28.7 us
  Pallas kernels  28.1 us (97%)
  between operations  0.64 us (2%)
    pallas_call x1, Pallas kernels, per_device(): pl.pallas_call(kernel, out_shape=(jax.ShapeDtypeStruct(tracers.shape, F32...  26.4 us
    pallas_call x1, Pallas kernels, per_device(): pl.pallas_call(write_out, out_shape=tuple((jax.ShapeDtypeStruct(a.shape,...  1.68 us

profile of v3, /device:TPU:0, one launch (start us, length us, event | category | flops | bytes accessed | tf_op | source)
XLA Modules:
  0.0 28.7 jit_solution(16453033170361921909)
XLA Ops:
  0.6 26.4 %shard_map.138 = (f32[2,40,512]{2,1,0:T(8,128)}, f32[40,512]{1,0:T(8,128)}, f32[4,128]{1,0:T(4,128)}, f32[4,512]{1,0:T(4,128)}) custom-call(f32[2,40,512]{2,1,0:T(8,128)} %tr_in.1, f32[40,512]{1,0:T(8,128)} %th_in.1, f32[4,128]{1,0:T(4,128)} %bitcast.11, f32[4,128]{1,0:T(4,128)} %bitcast.12, s32[6,512]{1,0:T(8,128)} %near_in.1, f32[6,512]{1,0:T(8,128)} %ew_in.1, ...), custom_call_target="tpu_custom_call" | custom-call | flops 1258291200 | bytes 655360 | tf_op jit(solution)/shard_map/pallas_call | solution.py:668
  27.0 1.7 %shard_map.139 = (f32[2,40,512]{2,1,0:T(8,128)}, f32[40,512]{1,0:T(8,128)}, f32[4,128]{1,0:T(4,128)}, f32[4,512]{1,0:T(4,128)}) custom-call(f32[2,40,512]{2,1,0:T(8,128)} %get-tuple-element.12.refs_0_, f32[40,512]{1,0:T(8,128)} %get-tuple-element.13.refs_1_, f32[4,128]{1,0:T(4,128)} %get-tuple-element.14.refs_2_, f32[4,512]{1,0:T(4,128)} %get-tuple-element.15.refs_3_), custom_call_target="tpu_custom_call" | custom-call | tf_op jit(solution)/shard_map/pallas_call | solution.py:743
